TPU v7x, 32 devices: a whole 2x2x4 slice. The times are simulated.
32 devices in a mesh: mol: 8 (over z, core), stream: 2 (over y), head: 2 (over x).
Axes of the slice: x: 2, y: 2, z: 4, core: 2. Of those that a mesh axis runs over, the one named last changes fastest.
Arguments:
- tokens: bfloat16 [8192, 768], P(('mol', 'stream')), may hold values from -6 to 6
- cotangent: float32 [8192, 768], P(('mol', 'stream')), may hold values from -6 to 6
- attn_gain: float32 [768], replicated, may hold values from 0.25 to 1.75
- attn_shift: float32 [768], replicated, may hold values from -2 to 2
- query_weight: bfloat16 [768, 768], P(None, 'head'), may hold values from -0.21875 to 0.21875
- query_bias: float32 [768], P('head'), may hold values from -3 to 3
- key_weight: bfloat16 [768, 768], P(None, 'head'), may hold values from -0.21875 to 0.21875
- value_weight: bfloat16 [768, 768], P(None, 'head'), may hold values from -0.21875 to 0.21875
- value_bias: float32 [768], P('head'), may hold values from -3 to 3
- out_weight: bfloat16 [768, 768], P('head'), may hold values from -0.875 to 0.875
- out_bias: float32 [768], replicated, may hold values from -3 to 3
- ffn_gain: float32 [768], replicated, may hold values from 0.25 to 1.75
- ffn_shift: float32 [768], replicated, may hold values from -2 to 2
- up_weight: bfloat16 [768, 768], P(None, 'head'), may hold values from -0.21875 to 0.21875
- up_bias: bfloat16 [768], P('head'), may hold values from -3 to 3
- down_weight: bfloat16 [768, 768], P('head'), may hold values from -0.3125 to 0.3125
- down_bias: float32 [768], replicated, may hold values from -3 to 3
- atom_counts: int32 [8, 16], P('mol'), may hold values from 1 to 24, 154 in all within a row
- edge_counts: int32 [8, 16], P('mol'), may hold values from 1 to 64, 512 in all within a row
Outputs:
- output: float32 [8192, 768], P(('mol', 'stream'))
- tokens_grad: float32 [8192, 768], P(('mol', 'stream'))
- attn_gain_grad: float32 [768], P('head')
- attn_shift_grad: float32 [768], P('head')
- query_weight_grad: float32 [768, 768], P(None, 'head')
- query_bias_grad: float32 [768], P('head')
- key_weight_grad: float32 [768, 768], P(None, 'head')
- value_weight_grad: float32 [768, 768], P(None, 'head')
- value_bias_grad: float32 [768], P('head')
- out_weight_grad: float32 [768, 768], P('head')
- out_bias_grad: float32 [768], P('head')
- ffn_gain_grad: float32 [768], P('head')
- ffn_shift_grad: float32 [768], P('head')
- up_weight_grad: float32 [768, 768], P(None, 'head')
- up_bias_grad: float32 [768], P('head')
- down_weight_grad: float32 [768, 768], P('head')
- down_bias_grad: float32 [768], P('head')
Inputs may be any that keep to these rules, and one draw needn't show every extreme that they name: `atom_counts`: A row holds the atom counts of the 16 molecules of one mol index; each row sums to exactly 154, and its largest entry is exactly 24. `edge_counts`: A row holds the edge token counts of the 16 molecules of one mol index; each row sums to exactly 512, and its largest entry is exactly 64.
All inputs are finite; a program needn't handle non-finite values.
Results may differ from a plain program's by a relative error of at most 0.013.
Values may be sent and summed in bfloat16 or wider, within the bound.
A program may use at most 256 MiB of HBM per device.

v0:
```python
import jax
import jax.numpy as jnp
from jax import lax
from jax.sharding import PartitionSpec as P

HEAD_DIM = 24


def plain_dot(operand, partner):
    return jnp.dot(operand, partner, preferred_element_type=jnp.float32)


def lead_dot(operand, partner):
    return lax.dot_general(
        operand, partner, (((0,), (0,)), ((), ())), preferred_element_type=jnp.float32
    )


def tail_dot(operand, partner):
    return lax.dot_general(
        operand, partner, (((1,), (1,)), ((), ())), preferred_element_type=jnp.float32
    )


def norm_apply(values, gain_vec, shift_vec):
    row_mean = jnp.mean(values, axis=-1, keepdims=True)
    centered = values - row_mean
    variance = jnp.mean(centered * centered, axis=-1, keepdims=True)
    return centered * lax.rsqrt(variance + 1e-05) * gain_vec + shift_vec


def gelu_exact(values):
    return jax.nn.gelu(values, approximate=False)


def segment_ids(counts, added, slot_count):
    seg_ends = jnp.cumsum(counts + added)
    positions = jnp.arange(slot_count, dtype=jnp.int32)
    return jnp.sum((positions[:, None] >= seg_ends[None, :]).astype(jnp.int32), axis=1)


def head_piece(vector, head_rank, head_share):
    return lax.dynamic_slice_in_dim(vector, head_rank * head_share, head_share)


def on_device(
    tokens,
    cotangent,
    attn_gain,
    attn_shift,
    query_weight,
    query_bias,
    key_weight,
    value_weight,
    value_bias,
    out_weight,
    out_bias,
    ffn_gain,
    ffn_shift,
    up_weight,
    up_bias,
    down_weight,
    down_bias,
    atom_counts,
    edge_counts,
):
    row_count = tokens.shape[0]
    model_width = tokens.shape[1]
    local_width = query_weight.shape[1]
    local_heads = local_width // HEAD_DIM
    head_count = lax.axis_size("head")
    head_rank = lax.axis_index("head")
    stream_rank = lax.axis_index("stream")
    molecules = atom_counts.shape[1]
    head_share = model_width // head_count
    score_scale = HEAD_DIM ** (-0.5)
    seg_node = segment_ids(atom_counts[0], 1, row_count)
    seg_edge = segment_ids(edge_counts[0], 0, row_count)
    key_seg = jnp.concatenate([seg_node, seg_edge])
    own_seg = jnp.where(stream_rank == 0, seg_node, seg_edge)
    live_rows = (own_seg < molecules).astype(jnp.float32)[:, None]
    residual = tokens.astype(jnp.float32)
    normed, norm_pull = jax.vjp(norm_apply, residual, attn_gain, attn_shift)
    first_in = normed.astype(jnp.bfloat16)
    queries = (plain_dot(first_in, query_weight) + query_bias).astype(jnp.bfloat16)
    keys_local = plain_dot(first_in, key_weight).astype(jnp.bfloat16)
    values_local = (plain_dot(first_in, value_weight) + value_bias).astype(jnp.bfloat16)
    all_keys, all_values = (
        lax.all_gather(keys_local, "stream", axis=0, tiled=True),
        lax.all_gather(values_local, "stream", axis=0, tiled=True),
    )
    key_count = all_keys.shape[0]
    key_heads = all_keys.reshape(key_count, local_heads, HEAD_DIM)
    value_heads = all_values.reshape(key_count, local_heads, HEAD_DIM)
    blocks = row_count // 512
    block_rows = row_count // blocks
    query_blocks = queries.reshape(blocks, block_rows, local_heads, HEAD_DIM)
    seg_blocks = own_seg.reshape(blocks, block_rows)

    def forward_block(pieces):
        query_part, seg_part = pieces
        scores = (
            jnp.einsum("qhd,khd->hqk", query_part, key_heads, preferred_element_type=jnp.float32)
            * score_scale
        )
        same_mol = (seg_part[:, None] == key_seg[None, :])[None]
        scores = jnp.where(same_mol, scores, -1e30)
        row_top = jnp.max(scores, axis=-1, keepdims=True)
        shifted = jnp.exp(scores - row_top)
        row_total = jnp.sum(shifted, axis=-1, keepdims=True)
        prob_low = (shifted / row_total).astype(jnp.bfloat16)
        attended_part = jnp.einsum(
            "hqk,khd->qhd", prob_low, value_heads, preferred_element_type=jnp.float32
        )
        return (attended_part.astype(jnp.bfloat16), (row_top + jnp.log(row_total))[..., 0])

    attended_blocks, lse_blocks = lax.map(forward_block, (query_blocks, seg_blocks))
    attended = attended_blocks.reshape(row_count, local_width)
    attn_sum = lax.psum(plain_dot(attended, out_weight), "head")
    middle = residual + live_rows * (attn_sum + out_bias)
    second, second_pull = jax.vjp(norm_apply, middle, ffn_gain, ffn_shift)
    second_in = second.astype(jnp.bfloat16)
    inner_pre = plain_dot(second_in, up_weight) + up_bias.astype(jnp.float32)
    activated, gelu_pull = jax.vjp(gelu_exact, inner_pre)
    hidden = activated.astype(jnp.bfloat16)
    ffn_sum = lax.psum(plain_dot(hidden, down_weight).astype(jnp.bfloat16), "head").astype(
        jnp.float32
    )
    output = middle + live_rows * (ffn_sum + down_bias)
    down_cot = (live_rows * cotangent).astype(jnp.bfloat16)
    down_weight_grad = lead_dot(hidden, down_cot)
    down_bias_full = jnp.sum(down_cot.astype(jnp.float32), axis=0)
    inner_grad = gelu_pull(tail_dot(down_cot, down_weight))[0].astype(jnp.bfloat16)
    up_weight_grad = lead_dot(second_in, inner_grad)
    up_bias_grad = jnp.sum(inner_grad.astype(jnp.float32), axis=0)
    second_grad = lax.psum(tail_dot(inner_grad, up_weight), "head")
    middle_part, ffn_gain_full, ffn_shift_full = second_pull(second_grad)
    mid_grad = cotangent + middle_part
    ffn_gain_grad = head_piece(ffn_gain_full, head_rank, head_share)
    ffn_shift_grad = head_piece(ffn_shift_full, head_rank, head_share)
    down_bias_grad = head_piece(down_bias_full, head_rank, head_share)
    attn_cot = (live_rows * mid_grad).astype(jnp.bfloat16)
    out_weight_grad = lead_dot(attended, attn_cot)
    out_bias_full = jnp.sum(attn_cot.astype(jnp.float32), axis=0)
    attended_grad = tail_dot(attn_cot, out_weight).astype(jnp.bfloat16)
    grad_blocks = attended_grad.reshape(blocks, block_rows, local_heads, HEAD_DIM)

    def backward_block(running, pieces):
        key_acc, value_acc = running
        query_part, seg_part, lse_part, grad_part = pieces
        scores = (
            jnp.einsum("qhd,khd->hqk", query_part, key_heads, preferred_element_type=jnp.float32)
            * score_scale
        )
        same_mol = (seg_part[:, None] == key_seg[None, :])[None]
        prob_full = jnp.where(same_mol, jnp.exp(scores - lse_part[..., None]), 0.0)
        prob_low = prob_full.astype(jnp.bfloat16)
        prob_grad = jnp.einsum(
            "qhd,khd->hqk", grad_part, value_heads, preferred_element_type=jnp.float32
        )
        row_delta = jnp.sum(prob_grad * prob_full, axis=-1, keepdims=True)
        score_grad = (prob_full * (prob_grad - row_delta)).astype(jnp.bfloat16)
        query_part_grad = (
            jnp.einsum("hqk,khd->qhd", score_grad, key_heads, preferred_element_type=jnp.float32)
            * score_scale
        )
        key_acc = (
            key_acc
            + jnp.einsum("hqk,qhd->khd", score_grad, query_part, preferred_element_type=jnp.float32)
            * score_scale
        )
        value_acc = value_acc + jnp.einsum(
            "hqk,qhd->khd", prob_low, grad_part, preferred_element_type=jnp.float32
        )
        return ((key_acc, value_acc), query_part_grad.astype(jnp.bfloat16))

    zero_keys = jnp.zeros((key_count, local_heads, HEAD_DIM), jnp.float32)
    (key_acc, value_acc), query_grads = lax.scan(
        backward_block, (zero_keys, zero_keys), (query_blocks, seg_blocks, lse_blocks, grad_blocks)
    )
    key_sum, value_sum = (
        lax.psum_scatter(
            key_acc.reshape(key_count, local_width), "stream", scatter_dimension=0, tiled=True
        ),
        lax.psum_scatter(
            value_acc.reshape(key_count, local_width), "stream", scatter_dimension=0, tiled=True
        ),
    )
    key_grad = key_sum.astype(jnp.bfloat16)
    value_grad = value_sum.astype(jnp.bfloat16)
    query_grad = query_grads.reshape(row_count, local_width)
    query_weight_grad = lead_dot(first_in, query_grad)
    query_bias_grad = jnp.sum(query_grad.astype(jnp.float32), axis=0)
    key_weight_grad = lead_dot(first_in, key_grad)
    value_weight_grad = lead_dot(first_in, value_grad)
    value_bias_grad = jnp.sum(value_grad.astype(jnp.float32), axis=0)
    first_part = (
        tail_dot(query_grad, query_weight)
        + tail_dot(key_grad, key_weight)
        + tail_dot(value_grad, value_weight)
    )
    first_grad = lax.psum(first_part.astype(jnp.bfloat16), "head").astype(jnp.float32)
    resid_part, attn_gain_full, attn_shift_full = norm_pull(first_grad)
    tokens_grad = mid_grad + resid_part
    attn_gain_grad = head_piece(attn_gain_full, head_rank, head_share)
    attn_shift_grad = head_piece(attn_shift_full, head_rank, head_share)
    out_bias_grad = head_piece(out_bias_full, head_rank, head_share)
    (
        attn_gain_grad,
        attn_shift_grad,
        query_weight_grad,
        query_bias_grad,
        key_weight_grad,
        value_weight_grad,
        value_bias_grad,
        out_weight_grad,
        out_bias_grad,
        ffn_gain_grad,
        ffn_shift_grad,
        up_weight_grad,
        up_bias_grad,
        down_weight_grad,
        down_bias_grad,
    ) = lax.psum(
        (
            attn_gain_grad,
            attn_shift_grad,
            query_weight_grad,
            query_bias_grad,
            key_weight_grad,
            value_weight_grad,
            value_bias_grad,
            out_weight_grad,
            out_bias_grad,
            ffn_gain_grad,
            ffn_shift_grad,
            up_weight_grad,
            up_bias_grad,
            down_weight_grad,
            down_bias_grad,
        ),
        ("mol", "stream"),
    )
    return (
        output,
        tokens_grad,
        attn_gain_grad,
        attn_shift_grad,
        query_weight_grad,
        query_bias_grad,
        key_weight_grad,
        value_weight_grad,
        value_bias_grad,
        out_weight_grad,
        out_bias_grad,
        ffn_gain_grad,
        ffn_shift_grad,
        up_weight_grad,
        up_bias_grad,
        down_weight_grad,
        down_bias_grad,
    )


def solution(mesh):
    in_specs = (
        P(("mol", "stream"), None),
        P(("mol", "stream"), None),
        P(),
        P(),
        P(None, "head"),
        P("head"),
        P(None, "head"),
        P(None, "head"),
        P("head"),
        P("head", None),
        P(),
        P(),
        P(),
        P(None, "head"),
        P("head"),
        P("head", None),
        P(),
        P("mol", None),
        P("mol", None),
    )
    out_specs = (
        P(("mol", "stream"), None),
        P(("mol", "stream"), None),
        P("head"),
        P("head"),
        P(None, "head"),
        P("head"),
        P(None, "head"),
        P(None, "head"),
        P("head"),
        P("head", None),
        P("head"),
        P("head"),
        P("head"),
        P(None, "head"),
        P("head"),
        P("head", None),
        P("head"),
    )
    return jax.shard_map(
        on_device, mesh=mesh, in_specs=in_specs, out_specs=out_specs, check_vma=False
    )
```

profile of v0, /device:TPU:0, one launch (start us, length us, event | category | flops | bytes accessed | tf_op | source)
XLA Modules:
  0.0 557.2 jit_solution(575553935829346988)
XLA Ops:
  7.3 0.8 copy.47
  8.3 0.7 add_bitcast_fusion
  9.3 1.4 convert_reduce_fusion.1
  10.7 1.5 fusion.14
  12.8 0.6 fusion.17
  13.4 12.9 %all_gather.6 = bf16[1024,384]{1,0:T(8,128)(2,1)S(1)} all-gather(bf16[512,384]{1,0:T(8,128)(2,1)S(1)} %fusion.17), channel_id=1, replica_groups=mesh['mol'=8,'stream'=2,'head'=2] {'stream'}, dimensions={0}, use_global_device_ids=true | all-gather | bytes 1179648 | tf_op jit(solution)/shard_map/all_gather | solution.py:90
  26.3 1.2 copy.48
  27.5 0.6 convolution_convert_fusion.2
  28.1 11.1 %all_gather.7 = bf16[1024,384]{1,0:T(8,128)(2,1)} all-gather(bf16[512,384]{1,0:T(8,128)(2,1)S(1)} %convolution_convert_fusion.2), channel_id=1, replica_groups=mesh['mol'=8,'stream'=2,'head'=2] {'stream'}, dimensions={0}, use_global_device_ids=true | all-gather | bytes 1179648 | tf_op jit(solution)/shard_map/all_gather | solution.py:89
  39.2 1.4 copy.49
  41.0 1.6 fusion.18
  42.6 13.9 %select_reduce_fusion = (f32[16,512]{1,0:T(8,128)S(1)}, f32[16,512,1024]{2,1,0:T(8,128)}) fusion(pred[512,1024]{1,0:T(8,128)(4,1)S(1)} %broadcast_compare_fusion, bf16[512,16,24]{0,2,1:T(8,128)(2,1)S(1)} %bitcast.67, bf16[1024,16,24]{0,2,1:T(8,128)(2,1)S(1)} %bitcast.62), kind=kOutput, calls=%fused_computation.5 | convolution fusion | flops 427810816 | bytes 35291136 | tf_op jit(solution)/shard_map/while/body/eval_jaxpr/qhd,khd->hqk/dot_general | solution.py:103
  56.5 15.1 %fusion = f32[16,512]{1,0:T(8,128)S(1)} fusion(f32[16,512,1024]{2,1,0:T(8,128)} %get-tuple-element.114, f32[16,512]{1,0:T(8,128)S(1)} %get-tuple-element.113, pred[512,1024]{1,0:T(8,128)(4,1)S(1)} %broadcast_compare_fusion), kind=kLoop, calls=%fused_computation.6 | loop fusion | flops 33546240 | bytes 34144256 | tf_op jit(solution)/shard_map/while/body/eval_jaxpr/reduce_sum | solution.py:110
  71.6 13.9 %fusion.20 = bf16[16,24,512]{2,1,0:T(8,128)(2,1)S(1)} fusion(bf16[1024,16,24]{0,2,1:T(8,128)(2,1)S(1)} %bitcast.65, f32[16,512,1024]{2,1,0:T(8,128)} %get-tuple-element.114, f32[16,512]{1,0:T(8,128)S(1)} %fusion, f32[16,512]{1,0:T(8,128)S(1)} %get-tuple-element.113, pred[512,1024]{1,0:T(8,128)(4,1)S(1)} %broadcast_compare_fusion), kind=kOutput, calls=%fused_computation.53 | convolution fusion | flops 444792832 | bytes 35323904 | tf_op jit(solution)/shard_map/while/body/eval_jaxpr/hqk,khd->qhd/dot_general | solution.py:112
  85.5 1.7 fusion.44
  87.6 52.4 %all-reduce.8.cloned.1.call-done = f32[512,768]{1,0:T(8,128)} async-done(((f32[512,768]{1,0:T(8,128)}), f32[512,768]{1,0:T(8,128)}) %all-reduce.8.cloned.1.call-update) | async-done | bytes 1572880 | tf_op jit(solution)/shard_map/psum | solution.py:119
  140.0 3.0 convert_reduce_fusion.2
  144.4 0.6 convolution_add_fusion
  145.1 3.7 convert_reduce_fusion.4
  148.7 0.7 copy-done.25
  149.5 1.7 fusion.45
  151.3 0.8 log_add_fusion
  152.1 50.8 %all-reduce.10.cloned.1.call-done = f32[512,768]{1,0:T(8,128)} async-done(((f32[512,768]{1,0:T(8,128)}), f32[512,768]{1,0:T(8,128)}) %all-reduce.10.cloned.1.call-update) | async-done | bytes 1572880 | tf_op jit(solution)/shard_map/psum | solution.py:136
  202.9 2.7 multiply_reduce_fusion.1
  205.7 0.6 fusion.42
  206.3 0.7 copy-done.2
  207.5 0.6 copy-done.35
  208.9 24.8 %multiply_reduce_fusion = (f32[16,512]{1,0:T(8,128)S(1)}, f32[16,512,1024]{2,1,0:T(8,128)}) fusion(f32[16,512,1024]{2,1,0:T(8,128)} %get-tuple-element.114, f32[16,512]{1,0:T(8,128)S(1)} %log_add_fusion, pred[512,1024]{1,0:T(8,128)(4,1)S(1)} %broadcast_compare_fusion, bf16[512,16,24]{0,2,1:T(8,128)(2,1)S(1)} %bitcast.74, bf16[1024,16,24]{0,2,1:T(8,128)(2,1)S(1)} %bitcast.66), kind=kOutput, calls=%fused_computation.1 | convolution fusion | flops 444588032 | bytes 68878336 | tf_op jit(solution)/shard_map/while/body/eval_jaxpr/qhd,khd->hqk/dot_general | solution.py:158
  233.8 27.7 %multiply_convert_fusion = bf16[16,512,1024]{2,1,0:T(8,128)(2,1)} fusion(f32[16,512,1024]{2,1,0:T(8,128)} %get-tuple-element.116, f32[16,512,1024]{2,1,0:T(8,128)} %get-tuple-element.114, f32[16,512]{1,0:T(8,128)S(1)} %get-tuple-element.115, f32[16,512]{1,0:T(8,128)S(1)} %log_add_fusion, pred[512,1024]{1,0:T(8,128)(4,1)S(1)} %broadcast_compare_fusion), kind=kLoop, calls=%fused_computation | loop fusion | flops 50331648 | bytes 84475904 | tf_op jit(solution)/shard_map/while/body/eval_jaxpr/convert_element_type | solution.py:162
  261.4 9.4 %convolution_multiply_fusion = f32[16,24,1024]{2,1,0:T(8,128)} fusion(bf16[512,16,24]{0,2,1:T(8,128)(2,1)} %bitcast.68, bf16[16,512,1024]{2,1,0:T(8,128)(2,1)} %multiply_convert_fusion), kind=kOutput, calls=%fused_computation.42 | convolution fusion | flops 403046400 | bytes 18743296 | tf_op jit(solution)/shard_map/while/body/eval_jaxpr/hqk,qhd->khd/dot_general | solution.py:169
  270.9 15.4 %fusion.2 = f32[16,24,1024]{2,1,0:T(8,128)} fusion(bf16[512,16,24]{0,2,1:T(8,128)(2,1)} %bitcast.75, f32[16,512,1024]{2,1,0:T(8,128)} %get-tuple-element.114, f32[16,512]{1,0:T(8,128)S(1)} %log_add_fusion, pred[512,1024]{1,0:T(8,128)(4,1)S(1)} %broadcast_compare_fusion), kind=kOutput, calls=%fused_computation.8 | convolution fusion | flops 436207616 | bytes 36077568 | tf_op jit(solution)/shard_map/while/body/eval_jaxpr/hqk,qhd->khd/dot_general | solution.py:172
  286.3 9.0 %all-reduce.14.cloned.1.call-start = ((), (), s32[]{:S(2)}) async-start(), calls=%async_computation.7 | async-start | bytes 3145728 | tf_op jit(solution)/shard_map/psum | solution.py:126
  295.3 1.5 multiply_convert_fusion.3
  296.8 1.5 convolution_convert_fusion
  298.3 11.3 %convert_reduce_fusion.6 = (f32[16,24]{1,0:T(8,128)S(1)}, bf16[16,24,512]{2,1,0:T(8,128)(2,1)}) fusion(bf16[1024,16,24]{0,2,1:T(8,128)(2,1)} %bitcast.63, bf16[16,512,1024]{2,1,0:T(8,128)(2,1)} %multiply_convert_fusion), kind=kOutput, calls=%fused_computation.60 | convolution fusion | flops 403439232 | bytes 17958400 | tf_op jit(solution)/shard_map/while/body/eval_jaxpr/hqk,khd->qhd/dot_general | solution.py:164
  309.5 2.9 fusion.46
  312.5 3.1 fusion.30
  315.6 9.8 %reduce-scatter.5.cloned.1.call-done = f32[512,384]{0,1:T(8,128)} async-done(((f32[1024,384]{0,1:T(8,128)}), f32[512,384]{0,1:T(8,128)}) %reduce-scatter.5.cloned.1.call-update) | async-done | bytes 786448 | tf_op jit(solution)/shard_map/reduce_scatter | solution.py:185
  325.3 3.8 add_convert_fusion
  329.2 2.9 fusion.49
  332.2 1.5 fusion.50
  333.7 1.6 fusion.47
  335.3 1.5 fusion.48
  336.8 1.6 fusion.28
  338.5 1.6 fusion.34
  340.2 0.6 copy-done.52
  341.2 1.3 convert_reduce_fusion.5
  342.4 38.6 %all-reduce.14.cloned.1.call-done = (bf16[512,768]{1,0:T(8,128)(2,1)}, bf16[512,768]{1,0:T(8,128)(2,1)}) async-done(((bf16[512,768]{1,0:T(8,128)(2,1)}, bf16[512,768]{1,0:T(8,128)(2,1)}), (bf16[512,768]{1,0:T(8,128)(2,1)}, bf16[512,768]{1,0:T(8,128)(2,1)})) %all-reduce.14.cloned.1.call-update) | async-done | bytes 1572880 | tf_op jit(solution)/shard_map/psum | solution.py:126
  381.0 1.8 convert_reduce_fusion
  382.8 0.9 fusion.16
  383.9 64.0 %all-reduce = (f32[384]{0:T(512)}, f32[384]{0:T(512)}, f32[384]{0:T(512)}, f32[384]{0:T(512)}, f32[384]{0:T(512)}, /*index=5*/f32[384]{0:T(512)}, f32[384]{0:T(512)}, f32[384]{0:T(512)}, f32[384]{0:T(512)}) all-reduce(f32[384]{0:T(512)S(1)} %dynamic_slice.33, ...), channel_id=1, replica_groups=mesh['mol'=8,'stream'=2,'head'=2] {'mol','stream'}, use_global_device_ids=true, to_apply=%region_22.23 | all-reduce | flops 3456 | bytes 27648 | tf_op jit(solution)/shard_map/psum | solution.py:224
  448.0 2.7 multiply_add_fusion
  450.7 1.9 add_add_fusion.2
  452.6 87.3 %all-reduce.12.cloned.1.call-done = (f32[768,384]{1,0:T(8,128)}, f32[768,384]{1,0:T(8,128)}, f32[768,384]{1,0:T(8,128)}, f32[384,768]{1,0:T(8,128)}, f32[768,384]{1,0:T(8,128)}, /*index=5*/f32[384,768]{1,0:T(8,128)}) async-done(((f32[768,384]{1,0:T(8,128)}, f32[768,384]{1,0:T(8,128)}, f32[768,384]{1,0:T(8,128)}, f32[384,768]{1,0:T(8,128)}, f32[768,384]{1,0:T(8,128)}, /*index=5*/f32[384,768]{1,0:T(8,128)}), ...) | async-done | bytes 7077904 | tf_op jit(solution)/shard_map/psum | solution.py:224
  539.9 2.5 copy.60
  542.4 1.0 copy.61
  543.4 0.7 copy-done.29
  544.1 1.0 copy.62
  545.1 0.7 copy-done.28
  545.8 1.0 copy.63
  546.8 0.7 copy-done.27
  547.4 1.0 copy.64
  548.5 0.7 copy-done.26
  549.1 1.0 copy.65
  (156 shorter events, 5.4 us)
Async XLA Ops:
  7.2 137.9 %copy-start = (bf16[384,768]{1,0:T(8,128)(2,1)S(1)}, bf16[384,768]{1,0:T(8,128)(2,1)}, u32[]{:S(2)}) copy-start(bf16[384,768]{1,0:T(8,128)(2,1)} %param.34) | copy-start | bytes 1769476
  7.2 5.0 copy-start.1
  7.2 5.0 copy-start.53
  7.2 5.0 copy-start.41
  7.2 132.8 %all-reduce.8.cloned.1.call-start = ((), (), s32[]{:S(2)}) async-start(), calls=%async_computation.2 | async-start | bytes 3145728 | tf_op jit(solution)/shard_map/psum | solution.py:119
  9.3 3.5 copy-start.37
  9.3 3.5 copy-start.59
  10.7 1.9 copy-start.39
  12.8 28.1 %copy-start.6 = (bf16[512,768]{1,0:T(8,128)(2,1)}, bf16[512,768]{1,0:T(8,128)(2,1)S(1)}, u32[]{:S(2)}) copy-start(bf16[512,768]{1,0:T(8,128)(2,1)S(1)} %fusion.13) | copy-start | bytes 2359300
  13.4 14.1 %copy-start.36 = (bf16[768,384]{1,0:T(8,128)(2,1)S(1)}, bf16[768,384]{1,0:T(8,128)(2,1)}, u32[]{:S(2)}) copy-start(bf16[768,384]{1,0:T(8,128)(2,1)} %param.25) | copy-start | bytes 1769476
  28.1 12.9 %copy-start.60 = (f32[384]{0:T(512)S(1)}, f32[384]{0:T(512)}, u32[]{:S(2)}) copy-start(f32[384]{0:T(512)} %param.24) | copy-start | bytes 4612
  40.6 15.9 %copy-start.8 = (bf16[1024,384]{0,1:T(8,128)(2,1)}, bf16[1024,384]{0,1:T(8,128)(2,1)S(1)}, u32[]{:S(2)}) copy-start(bf16[1024,384]{0,1:T(8,128)(2,1)S(1)} %copy.49) | copy-start | bytes 2359300
  42.6 13.9 %copy-start.15 = (bf16[512,384]{0,1:T(8,128)(2,1)}, bf16[512,384]{0,1:T(8,128)(2,1)S(1)}, u32[]{:S(2)}) copy-start(bf16[512,384]{0,1:T(8,128)(2,1)S(1)} %fusion.18) | copy-start | bytes 1179652
  56.5 15.1 %copy-start.13 = (bf16[1024,384]{0,1:T(8,128)(2,1)S(1)}, bf16[1024,384]{0,1:T(8,128)(2,1)}, u32[]{:S(2)}) copy-start(bf16[1024,384]{0,1:T(8,128)(2,1)} %copy.48) | copy-start | bytes 2359300
  71.5 13.9 %copy-start.38 = (f32[16,512]{1,0:T(8,128)}, f32[16,512]{1,0:T(8,128)S(1)}, u32[]{:S(2)}) copy-start(f32[16,512]{1,0:T(8,128)S(1)} %fusion) | copy-start | bytes 98308
  71.5 13.9 %copy-start.34 = (bf16[384,768]{1,0:T(8,128)(2,1)S(1)}, bf16[384,768]{1,0:T(8,128)(2,1)}, u32[]{:S(2)}) copy-start(bf16[384,768]{1,0:T(8,128)(2,1)} %param.28) | copy-start | bytes 1769476
  85.5 1.8 copy-start.23
  85.5 2.1 copy-start.58
  85.5 54.6 %copy-start.55 = (f32[768]{0:T(1024)S(1)}, f32[768]{0:T(1024)}, u32[]{:S(2)}) copy-start(f32[768]{0:T(1024)} %param.29) | copy-start | bytes 9220
  87.3 115.6 %all-reduce.10.cloned.1.call-start = ((), (), s32[]{:S(2)}) async-start(), calls=%async_computation.3 | async-start | bytes 3145728 | tf_op jit(solution)/shard_map/psum | solution.py:136
  143.0 2.0 copy-start.19
  143.0 0.7 copy-start.43
  143.1 0.7 copy-start.54
  143.4 1.7 copy-start.48
  143.4 1.1 copy-start.33
  144.4 4.3 copy-start.17
  145.0 3.7 copy-start.32
  148.7 0.7 copy-start.25
  151.2 161.2 %reduce-scatter.3.cloned.1.call-start = ((), (), s32[]{:S(2)}) async-start(), calls=%async_computation.4 | async-start | bytes 2359296 | tf_op jit(solution)/shard_map/reduce_scatter | solution.py:182
  152.1 53.6 %copy-start.49 = (f32[512]{0:T(512)S(1)}, f32[512]{0:T(512)}, u32[]{:S(2)}) copy-start(f32[512]{0:T(512)} %copy-done.48) | copy-start | bytes 6148
  202.9 2.8 copy-start.12
  205.6 1.4 copy-start.2
  206.3 1.2 copy-start.4
  207.1 1.1 copy-start.35
  207.5 26.3 %copy-start.21 = (bf16[512,768]{1,0:T(8,128)(2,1)}, bf16[512,768]{1,0:T(8,128)(2,1)S(1)}, u32[]{:S(2)}) copy-start(bf16[512,768]{1,0:T(8,128)(2,1)S(1)} %get-tuple-element.104) | copy-start | bytes 2359300
  207.5 1.5 copy-start.14
  208.6 25.1 %copy-start.31 = (bf16[512,384]{0,1:T(8,128)(2,1)}, bf16[512,384]{0,1:T(8,128)(2,1)S(1)}, u32[]{:S(2)}) copy-start(bf16[512,384]{0,1:T(8,128)(2,1)S(1)} %convolution_convert_fusion.1) | copy-start | bytes 1179652
  270.8 54.5 %reduce-scatter.5.cloned.1.call-start = ((), (), s32[]{:S(2)}) async-start(), calls=%async_computation.5 | async-start | bytes 2359296 | tf_op jit(solution)/shard_map/reduce_scatter | solution.py:185
  286.3 94.7 %all-reduce.14.cloned.1.call-start = ((), (), s32[]{:S(2)}) async-start(), calls=%async_computation.7 | async-start | bytes 3145728 | tf_op jit(solution)/shard_map/psum | solution.py:126
  329.2 210.7 %all-reduce.12.cloned.1.call-start = ((), (), s32[]{:S(2)}) async-start(), calls=%async_computation.6 | async-start | bytes 14155776 | tf_op jit(solution)/shard_map/psum | solution.py:224
  329.2 2.9 copy-start.20
  332.2 1.5 copy-start.7
  332.2 1.5 copy-start.16
  333.7 1.6 copy-start.22
  333.7 1.6 copy-start.24
  335.3 1.5 copy-start.18
  336.8 1.6 copy-start.11
  340.1 0.9 copy-start.51
  340.1 1.0 copy-start.50
  340.1 40.9 %copy-start.40 = (f32[512]{0:T(512)S(1)}, f32[512]{0:T(512)}, u32[]{:S(2)}) copy-start(f32[512]{0:T(512)} %copy-done.39) | copy-start | bytes 6148
  340.1 40.9 %copy-start.42 = (f32[768]{0:T(1024)S(1)}, f32[768]{0:T(1024)}, u32[]{:S(2)}) copy-start(f32[768]{0:T(1024)} %param.21) | copy-start | bytes 9220
  340.1 42.6 %copy-start.47 = (f32[512]{0:T(512)S(1)}, f32[512]{0:T(512)}, u32[]{:S(2)}) copy-start(f32[512]{0:T(512)} %copy-done.46) | copy-start | bytes 6148
  340.1 42.7 %copy-start.45 = (f32[512]{0:T(512)S(1)}, f32[512]{0:T(512)}, u32[]{:S(2)}) copy-start(f32[512]{0:T(512)} %copy-done.44) | copy-start | bytes 6148
  381.0 1.8 copy-start.9
  381.0 2.9 copy-start.57
  381.0 67.0 %copy-start.56 = (f32[768]{0:T(1024)S(1)}, f32[768]{0:T(1024)}, u32[]{:S(2)}) copy-start(f32[768]{0:T(1024)} %param.35) | copy-start | bytes 9220
  448.0 2.7 copy-start.3
  448.0 2.7 copy-start.5
  448.0 2.7 copy-start.10
  539.9 2.5 copy-start.30
  542.4 1.7 copy-start.29
  544.1 1.7 copy-start.28
  545.8 1.7 copy-start.27
  547.4 1.7 copy-start.26
  (3 other events, 1.8 us)
Sparse Core Ops, SparseCore 0:
  87.4 52.6 all-reduce.7
  151.4 51.4 all-reduce.9
  270.9 26.0 reduce-scatter.2
  299.2 26.0 reduce-scatter.4
  329.3 51.6 all-reduce.13
  386.9 152.9 all-reduce.11
where the time goes:
time: 566 us; the launch traced here: 557 us
  waiting for transfers between devices  239 us (42%)
  matrix products  122 us (22%)
  blocking collectives  88 us (16%)
  other arithmetic  65.5 us (12%)
  local copies, waits for them, and re-layouts  18.6 us (3%)
  between operations  14.9 us (3%)
  starting transfers between devices  9.47 us (2%)
    psum x1, waiting for transfers between devices, on_device(): lax.psum((attn_gain_grad, attn_shift_grad, query_weight_grad, query_bias_...  87.3 us
    psum x1, blocking collectives, on_device(): lax.psum((attn_gain_grad, attn_shift_grad, query_weight_grad, query_bias_...  64 us
    psum x1, waiting for transfers between devices, on_device(): attn_sum = lax.psum(plain_dot(attended, out_weight), 'head')  52.4 us
    psum x1, waiting for transfers between devices, on_device(): second_grad = lax.psum(tail_dot(inner_grad, up_weight), 'head')  50.8 us
    psum x1, waiting for transfers between devices, on_device(): lax.psum(plain_dot(hidden, down_weight).astype(jnp.bfloat16), 'head')  38.6 us
    convert_element_type x1, other arithmetic, backward_block(): score_grad = (prob_full * (prob_grad - row_delta)).astype(jnp.bfloat16)  27.7 us
    dot_general x1, matrix products, backward_block(): jnp.einsum('qhd,khd->hqk', grad_part, value_heads, preferred_element_type...  24.8 us
    dot_general x6, matrix products, tail_dot(): lax.dot_general(operand, partner, (((1,), (1,)), ((), ())), preferred_ele...  15.7 us
  transfers between devices with their start and end apart: 6, of which 5 were waited for; matrix products, arithmetic and copies ran while one was open for 10% of the time, Pallas kernels for 0%

commit v1 on v0

--- a/solution.py
+++ b/solution.py
@@ -1,9 +1,819 @@
+import functools
+import math
+
 import jax
 import jax.numpy as jnp
 from jax import lax
+from jax.experimental import pallas as pl
+from jax.experimental.pallas import tpu as pltpu
 from jax.sharding import PartitionSpec as P
 
 HEAD_DIM = 24
+BF = jnp.bfloat16
+F32 = jnp.float32
+MESH = pl.DeviceIdType.MESH
+EDGES = 512
+NODES = 192
+TOTAL = EDGES + NODES
+PADDED = 768
+HEADS_HERE = 8
+SCALE = HEAD_DIM ** (-0.5)
+SCALE2 = SCALE * math.log2(math.e)
+BLOCKS = (
+    (0, 256, ((0, 384), (512, 256))),
+    (256, 256, ((128, 384), (512, 256))),
+    (512, 192, ((0, 768),)),
+)
+OWNERS = (((0, 0), 512, 192), ((1, 0), 0, 256), ((1, 1), 256, 256))
+
+
+def nn(a, b):
+    return jnp.dot(a, b, preferred_element_type=F32)
+
+
+def nt(a, b):
+    return lax.dot_general(a, b, (((1,), (1,)), ((), ())), preferred_element_type=F32)
+
+
+def tn(a, b):
+    return lax.dot_general(a, b, (((0,), (0,)), ((), ())), preferred_element_type=F32)
+
+
+def row_loop(count, step, fn, init):
+    def body(i, carry):
+        return fn(pl.ds(pl.multiple_of(i * step, step), step), carry)
+
+    return lax.fori_loop(0, count // step, body, init)
+
+
+def normed(x):
+    mu = jnp.mean(x, axis=-1, keepdims=True)
+    xc = x - mu
+    var = jnp.mean(xc * xc, axis=-1, keepdims=True)
+    r = lax.rsqrt(var + 1e-05)
+    return xc * r, r
+
+
+def col_sum(x):
+    return jnp.sum(x, axis=0, keepdims=True)
+
+
+SEM = {}
+
+
+def sem_id(name, count=1):
+    if name not in SEM:
+        SEM[name] = sum(n for _, n in SEM.values()), count
+    return SEM[name][0]
+
+
+N_SEMS = 96
+N_LOCAL = 24
+
+
+def layer_kernel(
+    tokens, cot, wq, wk, wv, wo, wu, wd,
+    atoms, edges,
+    a_gain, a_shift, q_bias, v_bias, o_bias, f_gain, f_shift, u_bias, d_bias,
+    d_out, d_tok, f1, f2, vec,
+    tok, res, cotv, ww, fwo, fwu, fwd, ub, fin1, qkv, dxw, qm, dam,
+    p0, p1, p2, bias, segc, attf, att, ain, da, delta,
+    t0, t1, n2s, r2s, mid, sec, hid, dc, ig, ac, ato, ago, mgd,
+    ds, dkf, dvf,
+    g1, gs1, qr, gq, zr1, g2, gs2, zr2, fp, fin,
+    vq, vz, vc,
+    ss, rs, ls,
+):
+    m, s, h = lax.axis_index("mol"), lax.axis_index("stream"), lax.axis_index("head")
+    z, c = m // 2, lax.rem(m, 2)
+    zc = lax.axis_size("mol") // 2
+    me = 2 * s + h
+    x_peer, y_peer, xy_peer = (m, s, 1 - h), (m, 1 - s, h), (m, 1 - s, 1 - h)
+    quad = (x_peer, y_peer, xy_peer)
+    twin = (2 * z + 1 - c, s, h)
+    z_peers = [(2 * lax.rem(z + d, zc) + c, s, h) for d in range(1, zc)]
+
+    def remote(name, src, dst, dev, k=0, count=1):
+        i = sem_id(name, count) + k
+        return pltpu.make_async_remote_copy(
+            src_ref=src, dst_ref=dst, send_sem=ss.at[i], recv_sem=rs.at[i],
+            device_id=dev, device_id_type=MESH,
+        )
+
+    def local(k, src, dst):
+        return pltpu.make_async_copy(src, dst, ls.at[k])
+
+    own = pl.multiple_of(256 * h, 256)
+    other = pl.multiple_of(256 * (1 - h), 256)
+    window = pl.multiple_of(128 * s, 128)
+
+    loads = [
+        local(0, tokens.at[pl.ds(own, 256)], res),
+        local(1, cot.at[pl.ds(own, 256)], cotv),
+        local(2, wq.at[:, pl.ds(window, 256)], ww.at[:, 0:256]),
+        local(3, wk.at[:, pl.ds(window, 256)], ww.at[:, 256:512]),
+        local(4, wv.at[:, pl.ds(window, 256)], ww.at[:, 512:768]),
+        local(5, wo, fwo.at[h]),
+        local(6, wu, fwu.at[h]),
+        local(7, wd, fwd.at[h]),
+    ]
+    edge_load = local(8, tokens, tok.at[0:EDGES])
+    node_load = local(9, tokens.at[0:NODES], tok.at[EDGES:TOTAL])
+    pl.when(s == 1)(edge_load.start)
+    pl.when(s == 0)(node_load.start)
+    for copy in loads:
+        copy.start()
+    ub[h] = jnp.broadcast_to(u_bias[...].astype(F32), (8, 384))
+
+    barrier = pltpu.get_barrier_semaphore()
+    greeted = [*quad, twin, *z_peers]
+    for dev in greeted:
+        pl.semaphore_signal(barrier, inc=1, device_id=dev, device_id_type=MESH)
+    pl.semaphore_wait(barrier, len(greeted))
+
+    def edge_part(k, half):
+        rows = pl.ds(pl.multiple_of(256 * half + 128 * k, 128), 128)
+        return rows
+
+    tok_y = [
+        remote("tok_y", tokens.at[edge_part(k, h)], tok.at[edge_part(k, h)], y_peer, k, 2)
+        for k in range(2)
+    ]
+    tok_x = [
+        remote("tok_x", tok.at[edge_part(k, h)], tok.at[edge_part(k, h)], x_peer, k, 2)
+        for k in range(2)
+    ]
+    tok_x_in = [
+        remote("tok_x", tok.at[edge_part(k, 1 - h)], tok.at[edge_part(k, 1 - h)], x_peer, k, 2)
+        for k in range(2)
+    ]
+    tok_n = remote("tok_n", tokens.at[0:NODES], tok.at[EDGES:TOTAL], y_peer)
+
+    @pl.when(s == 1)
+    def _():
+        for copy in tok_y:
+            copy.start()
+
+    pl.when(s == 0)(tok_n.start)
+    u_send = remote("ub", ub.at[h], ub.at[h], x_peer)
+    u_send.start()
+    part_o = pl.ds(pl.multiple_of(192 * c, 192), 192)
+    part_u = pl.ds(pl.multiple_of(384 * c, 384), 384)
+    w_out = [
+        remote("wo_x", wo.at[part_o], fwo.at[h, part_o], x_peer),
+        remote("wu_x", wu.at[part_u], fwu.at[h, part_u], x_peer),
+        remote("wd_x", wd.at[part_o], fwd.at[h, part_o], x_peer),
+    ]
+    for copy in w_out:
+        copy.start()
+    w_in = [
+        remote("wo_x", wo.at[part_o], fwo.at[1 - h, part_o], x_peer),
+        remote("wu_x", wu.at[part_u], fwu.at[1 - h, part_u], x_peer),
+        remote("wd_x", wd.at[part_o], fwd.at[1 - h, part_o], x_peer),
+    ]
+    w_twin = [
+        remote("wo_c", fwo.at[1 - h, part_o], fwo.at[1 - h, part_o], twin),
+        remote("wu_c", fwu.at[1 - h, part_u], fwu.at[1 - h, part_u], twin),
+        remote("wd_c", fwd.at[1 - h, part_o], fwd.at[1 - h, part_o], twin),
+    ]
+
+    def share_weight(k):
+        w_in[k].wait_recv()
+        w_twin[k].start()
+
+    def ends_of(counts, added):
+        total, ends = 0, []
+        for j in range(counts.shape[1]):
+            total = total + counts[0, j] + added
+            ends.append(total)
+        return ends
+
+    node_ends, edge_ends = ends_of(atoms, 1), ends_of(edges, 0)
+    live_count = jnp.where(s == 0, node_ends[-1], edge_ends[-1])
+
+    def seg_of(position, ends):
+        seg = jnp.zeros_like(position)
+        for end in ends:
+            seg = seg + jnp.where(position >= end, 1, 0)
+        return seg
+
+    segc[0:EDGES] = seg_of(lax.broadcasted_iota(jnp.int32, (EDGES, 1), 0), edge_ends)
+    segc[EDGES:TOTAL] = seg_of(lax.broadcasted_iota(jnp.int32, (NODES, 1), 0), node_ends)
+    at_row = lax.broadcasted_iota(jnp.int32, (1, PADDED), 1)
+    seg_r = jnp.where(at_row < EDGES, seg_of(at_row, edge_ends), seg_of(at_row - EDGES, node_ends))
+    seg_r = jnp.where(at_row < TOTAL, seg_r, -1)
+
+    lane = lax.broadcasted_iota(jnp.int32, (1, 256), 1) - 64 * s
+    head_of = jnp.where((lane >= 0) & (lane < 192), lane // HEAD_DIM, -1)
+    zero = jnp.zeros((), BF)
+
+    qkv[TOTAL:PADDED] = jnp.zeros((PADDED - TOTAL, 768), BF)
+    bias_row = jnp.concatenate(
+        [
+            q_bias[:, pl.ds(window, 256)],
+            jnp.zeros((1, 256), F32),
+            v_bias[:, pl.ds(window, 256)],
+        ],
+        axis=1,
+    )
+
+    def project(first, count):
+        def norm_rows(i, carry):
+            rows = pl.ds(pl.multiple_of(first + i * 64, 64), 64)
+            n1, _ = normed(tok[rows].astype(F32))
+            fin1[rows] = (n1 * a_gain[...] + a_shift[...]).astype(BF)
+            return carry
+
+        lax.fori_loop(0, count // 64, norm_rows, 0)
+        rows = pl.ds(pl.multiple_of(first, 64), count)
+        qkv[rows] = (nn(fin1[rows], ww[...]) + bias_row).astype(BF)
+
+    for copy in loads[2:5]:
+        copy.wait()
+
+    @pl.when(s == 1)
+    def _():
+        edge_load.wait()
+        project(0, EDGES)
+        tok_n.wait_recv()
+        project(EDGES, NODES)
+
+    @pl.when(s == 0)
+    def _():
+        node_load.wait()
+        project(EDGES, NODES)
+        for k in range(2):
+            tok_y[k].wait_recv()
+            tok_x[k].start()
+        project(own, 256)
+        for k in range(2):
+            tok_x_in[k].wait_recv()
+        project(other, 256)
+
+    for j in range(HEADS_HERE):
+        qm[j] = jnp.where(head_of == j, qkv[0:TOTAL, 0:256], zero)
+
+    def send_rows(name, src, dst, k):
+        dev_sh, first, count = OWNERS[k]
+        target = (m, *dev_sh)
+        mine = 2 * dev_sh[0] + dev_sh[1]
+
+        @pl.when(me != mine)
+        def _():
+            i = sem_id(name + "_s", 3) + k
+            j = sem_id(name, 4) + me
+            pltpu.make_async_remote_copy(
+                src_ref=src.at[first:first + count], dst_ref=dst.at[me, 0:count],
+                send_sem=ss.at[i], recv_sem=rs.at[j], device_id=target, device_id_type=MESH,
+            ).start()
+
+        @pl.when(me == mine)
+        def _():
+            dst[mine, 0:count] = src[first:first + count]
+
+    def wait_rows(name, src, dst):
+        for k, (dev_sh, first, count) in enumerate(OWNERS):
+            mine = 2 * dev_sh[0] + dev_sh[1]
+
+            @pl.when(me == mine)
+            def _():
+                for r in range(4):
+                    if r != mine:
+                        j = sem_id(name, 4) + r
+                        pltpu.make_async_remote_copy(
+                            src_ref=src.at[first:first + count], dst_ref=dst.at[r, 0:count],
+                            send_sem=ss.at[j], recv_sem=rs.at[j], device_id=x_peer, device_id_type=MESH,
+                        ).wait_recv()
+
+    def wait_sent(name, src, dst):
+        for k, (dev_sh, first, count) in enumerate(OWNERS):
+            mine = 2 * dev_sh[0] + dev_sh[1]
+
+            @pl.when(me != mine)
+            def _():
+                i = sem_id(name + "_s", 3) + k
+                pltpu.make_async_remote_copy(
+                    src_ref=src.at[first:first + count], dst_ref=dst.at[me, 0:count],
+                    send_sem=ss.at[i], recv_sem=rs.at[i], device_id=(m, *dev_sh), device_id_type=MESH,
+                ).wait_send()
+
+    def pick_heads(stacked, rows):
+        total = None
+        for j in range(HEADS_HERE):
+            part = jnp.where(head_of == j, stacked[j * rows:(j + 1) * rows], 0.0)
+            total = part if total is None else total + part
+        return total
+
+    probs = (p0, p1, p2)
+    to_owner = (1, 2, 0)
+    group = 2
+
+    @pl.when(s == 0)
+    def _():
+        ain[:, NODES:256] = jnp.zeros((4, 256 - NODES, 256), BF)
+        fin[:, NODES:256] = jnp.zeros((4, 256 - NODES, 768), BF)
+
+    @pl.when((s == 0) & (h == 1))
+    def _():
+        ain[:, 0:NODES] = jnp.zeros((4, NODES, 256), BF)
+        fin[:, 0:NODES] = jnp.zeros((4, NODES, 768), BF)
+
+    for b, (q0, qn, segs) in enumerate(BLOCKS):
+        o = 0
+        for a, n in segs:
+            bias[0:qn, o:o + n] = jnp.where(segc[q0:q0 + qn] == seg_r[:, a:a + n], 0.0, -1e30)
+            o += n
+        for j0 in range(0, HEADS_HERE, group):
+            qb = qm[j0:j0 + group, q0:q0 + qn, :].reshape(group * qn, 256)
+            raw = [nt(qb, qkv[a:a + n, 256:512]) for a, n in segs]
+            for g in range(group):
+                j, o, parts = j0 + g, 0, []
+                for piece, (a, n) in zip(raw, segs):
+                    parts.append(piece[g * qn:(g + 1) * qn] * SCALE2 + bias[0:qn, o:o + n])
+                    o += n
+                top = functools.reduce(
+                    jnp.maximum, [jnp.max(x, axis=1, keepdims=True) for x in parts]
+                )
+                parts = [jnp.exp2(x - top) for x in parts]
+                inv = 1.0 / sum(jnp.sum(x, axis=1, keepdims=True) for x in parts)
+                o = 0
+                for x, (a, n) in zip(parts, segs):
+                    probs[b][j * qn:(j + 1) * qn, o:o + n] = (x * inv).astype(BF)
+                    o += n
+        o, acc = 0, None
+        for a, n in segs:
+            part = nn(probs[b][:, o:o + n], qkv[a:a + n, 512:768])
+            acc = part if acc is None else acc + part
+            o += n
+        picked = pick_heads(acc, qn)
+        attf[q0:q0 + qn] = picked
+        att[q0:q0 + qn] = picked.astype(BF)
+        send_rows("att", att, ain, to_owner[b])
+
+    share_weight(0)
+    share_weight(1)
+
+    for copy in (loads[0], loads[1], *loads[5:8]):
+        copy.wait()
+    row_at = lax.broadcasted_iota(jnp.int32, (256, 1), 0) + own
+    live_all = jnp.where(row_at < live_count, 1.0, 0.0)
+    r2s[:, 1:2] = live_all
+    wait_rows("att", att, ain)
+    for x in range(2):
+        ato[:, 384 * x:384 * x + 128] = ain[x, :, 0:128]
+        ato[:, 384 * x + 128:384 * x + 256] = ain[x, :, 128:256] + ain[2 + x, :, 0:128]
+        ato[:, 384 * x + 256:384 * x + 384] = ain[2 + x, :, 128:256]
+    share_weight(2)
+    for copy in w_twin:
+        pass
+    twin_o = pl.ds(pl.multiple_of(192 * (1 - c), 192), 192)
+    twin_u = pl.ds(pl.multiple_of(384 * (1 - c), 384), 384)
+    w_twin_in = [
+        remote("wo_c", fwo.at[1 - h, twin_o], fwo.at[1 - h, twin_o], twin),
+        remote("wu_c", fwu.at[1 - h, twin_u], fwu.at[1 - h, twin_u], twin),
+        remote("wd_c", fwd.at[1 - h, twin_o], fwd.at[1 - h, twin_o], twin),
+    ]
+    w_twin_in[0].wait_recv()
+    wo_all = fwo[...].reshape(768, 768)
+    t0[...] = nn(ato[...], wo_all)
+    live_of = lambda rows: r2s[rows, 1:2]
+
+    def middle_rows(rows, carry):
+        x = res[rows].astype(F32) + live_of(rows) * (t0[rows] + o_bias[...])
+        mid[rows] = x
+        n2, r2 = normed(x)
+        n2s[rows] = n2
+        r2s[rows, 0:1] = r2
+        sec[rows] = (n2 * f_gain[...] + f_shift[...]).astype(BF)
+        return carry
+
+    row_loop(256, 64, middle_rows, 0)
+    w_twin_in[1].wait_recv()
+    u_recv = remote("ub", ub.at[1 - h], ub.at[1 - h], x_peer)
+    u_recv.wait_recv()
+    for x in range(2):
+        t0[:, 384 * x:384 * (x + 1)] = nn(sec[...], fwu[x]) + ub[x, 0:1]
+
+    def gelu_rows(rows, carry):
+        u = t0[rows]
+        cdf = 0.5 * (1.0 + lax.erf(u * math.sqrt(0.5)))
+        hid[rows] = (u * cdf).astype(BF)
+        t1[rows] = cdf + u * (jnp.exp(-0.5 * u * u) * (1.0 / math.sqrt(2.0 * math.pi)))
+        return carry
+
+    row_loop(256, 64, gelu_rows, 0)
+    w_twin_in[2].wait_recv()
+    wd_all = fwd[...].reshape(768, 768)
+    t0[...] = nn(hid[...], wd_all)
+    zero_row = jnp.zeros((1, 768), F32)
+
+    def out_rows(rows, carry):
+        live = live_of(rows)
+        x = (mid[rows] + live * (t0[rows] + d_bias[...])) - res[rows].astype(F32)
+        at = pl.ds(pl.multiple_of(own + rows.start, 64), 64)
+        d_out[at] = x.astype(BF)
+        down = (live * cotv[rows]).astype(BF)
+        dc[rows] = down
+        return carry + col_sum(down.astype(F32))
+
+    down_bias_sum = row_loop(256, 64, out_rows, zero_row)
+    own_rows = pl.ds(own, 256)
+    other_rows = pl.ds(other, 256)
+    out_send = remote("out", d_out.at[own_rows], d_out.at[own_rows], x_peer)
+    out_send.start()
+    t0[...] = nt(dc[...], wd_all)
+
+    def inner_rows(rows, carry):
+        x = (t0[rows] * t1[rows]).astype(BF)
+        ig[rows] = x
+        return carry + col_sum(x.astype(F32))
+
+    up_bias_sum = row_loop(256, 64, inner_rows, zero_row)
+    t0[...] = nt(ig[:, 0:384], fwu[0]) + nt(ig[:, 384:768], fwu[1])
+
+    def second_rows(rows, carry):
+        gain_sum, shift_sum, bias_sum = carry
+        sg, n2 = t0[rows], n2s[rows]
+        g = sg * f_gain[...]
+        back = r2s[rows, 0:1] * (
+            g - jnp.mean(g, axis=-1, keepdims=True) - n2 * jnp.mean(g * n2, axis=-1, keepdims=True)
+        )
+        mgd[rows] = back
+        x = (live_of(rows) * (cotv[rows] + back)).astype(BF)
+        ac[rows] = x
+        return gain_sum + col_sum(sg * n2), shift_sum + col_sum(sg), bias_sum + col_sum(x.astype(F32))
+
+    f_gain_sum, f_shift_sum, out_bias_sum = row_loop(
+        256, 64, second_rows, (zero_row, zero_row, zero_row)
+    )
+    ago[...] = nt(ac[...], wo_all).astype(BF)
+
+    for k, (dev_sh, first, count) in enumerate(OWNERS):
+        mine = 2 * dev_sh[0] + dev_sh[1]
+
+        @pl.when(me == mine)
+        def _():
+            for r in range(4):
+                cols = slice(384 * (r % 2) + 128 * (r // 2), 384 * (r % 2) + 128 * (r // 2) + 256)
+                if r == mine:
+                    da[first:first + count] = ago[0:count, cols]
+                else:
+                    i, j = sem_id("da_s", 4) + r, sem_id("da", 3) + k
+                    pltpu.make_async_remote_copy(
+                        src_ref=ago.at[0:count, cols], dst_ref=da.at[first:first + count],
+                        send_sem=ss.at[i], recv_sem=rs.at[j],
+                        device_id=(m, r // 2, r % 2), device_id_type=MESH,
+                    ).start()
+
+    for cc in range(2):
+        for xh in range(2):
+            f = slice(384 * xh, 384 * (xh + 1))
+            d = slice(384 * cc, 384 * (cc + 1))
+            g1[cc, xh, 0:384] = tn(hid[:, f], dc[:, d]).astype(BF)
+            g1[cc, xh, 384:768] = tn(ato[:, f], ac[:, d]).astype(BF)
+            g1[cc, xh, 768:1152] = tn(sec[:, d], ig[:, f]).astype(BF)
+    g1_twin = remote("g1_c", g1.at[1 - c], gs1, twin)
+    g1_twin.start()
+    g1_twin.wait_recv()
+
+    def twin_sum(i, carry):
+        rows = pl.ds(pl.multiple_of(i * 64, 64), 64)
+        for xh in range(2):
+            gs1[xh, rows] = (g1[c, xh, rows].astype(F32) + gs1[xh, rows].astype(F32)).astype(BF)
+        return carry
+
+    lax.fori_loop(0, 1152 // 64, twin_sum, 0)
+    half_of = lambda t: pl.ds(pl.multiple_of(576 * t, 576), 576)
+    g1_quad = [
+        remote("g1_q", gs1.at[1 - h, half_of(s)], qr.at[0], x_peer, 0, 3),
+        remote("g1_q", gs1.at[h, half_of(1 - s)], qr.at[1], y_peer, 1, 3),
+        remote("g1_q", gs1.at[1 - h, half_of(1 - s)], qr.at[2], xy_peer, 2, 3),
+    ]
+    for copy in g1_quad:
+        copy.start()
+
+    for k, (dev_sh, first, count) in enumerate(OWNERS):
+        mine = 2 * dev_sh[0] + dev_sh[1]
+
+        @pl.when(me != mine)
+        def _():
+            j = sem_id("da", 3) + k
+            pltpu.make_async_remote_copy(
+                src_ref=ago.at[0:count, 0:256], dst_ref=da.at[first:first + count],
+                send_sem=ss.at[j], recv_sem=rs.at[j], device_id=x_peer, device_id_type=MESH,
+            ).wait_recv()
+
+    head_col = lax.broadcasted_iota(jnp.int32, (256, 128), 1)
+    lane_row = lax.broadcasted_iota(jnp.int32, (256, 128), 0) - 64 * s
+    head_pick = jnp.where(
+        (lane_row >= 0) & (lane_row < 192) & (lane_row // HEAD_DIM == head_col), 1.0, 0.0
+    ).astype(BF)
+    prod = da[0:TOTAL].astype(F32) * attf[...]
+    prod_hi = prod.astype(BF)
+    delta[...] = nn(prod_hi, head_pick) + nn((prod - prod_hi.astype(F32)).astype(BF), head_pick)
+    for j in range(HEADS_HERE):
+        dam[j] = jnp.where(head_of == j, da[0:TOTAL], zero)
+    dkf[...] = jnp.zeros_like(dkf)
+    dvf[...] = jnp.zeros_like(dvf)
+    for b, (q0, qn, segs) in enumerate(BLOCKS):
+        pr = probs[b]
+        for j0 in range(0, HEADS_HERE, group):
+            ab = dam[j0:j0 + group, q0:q0 + qn, :].reshape(group * qn, 256)
+            o = 0
+            for a, n in segs:
+                pg = nt(ab, qkv[a:a + n, 512:768])
+                for g in range(group):
+                    j = j0 + g
+                    r = slice(j * qn, (j + 1) * qn)
+                    ds[r, o:o + n] = (
+                        pr[r, o:o + n].astype(F32)
+                        * (pg[g * qn:(g + 1) * qn] - delta[q0:q0 + qn, j:j + 1])
+                    ).astype(BF)
+                o += n
+        o, acc = 0, None
+        for a, n in segs:
+            part = nn(ds[0:HEADS_HERE * qn, o:o + n], qkv[a:a + n, 256:512])
+            acc = part if acc is None else acc + part
+            o += n
+        dxw[q0:q0 + qn, 0:256] = (pick_heads(acc, qn) * SCALE).astype(BF)
+        o = 0
+        for a, n in segs:
+            dk = dv = None
+            for j in range(HEADS_HERE):
+                r = slice(j * qn, (j + 1) * qn)
+                pk = tn(ds[r, o:o + n], qm[j, q0:q0 + qn])
+                pv = tn(pr[r, o:o + n], dam[j, q0:q0 + qn])
+                dk = pk if dk is None else dk + pk
+                dv = pv if dv is None else dv + pv
+            dkf[a:a + n] += dk
+            dvf[a:a + n] += dv
+            o += n
+    dxw[:, 256:512] = (dkf[0:TOTAL] * SCALE).astype(BF)
+    dxw[:, 512:768] = dvf[0:TOTAL].astype(BF)
+
+    for k in (1, 2, 0):
+        _, first, count = OWNERS[k]
+        fp[first:first + count] = nt(dxw[first:first + count], ww[...]).astype(BF)
+        send_rows("fp", fp, fin, k)
+
+    for cc in range(2):
+        g2[cc] = tn(fin1[0:TOTAL, 384 * cc:384 * (cc + 1)], dxw[...]).astype(BF)
+    g2_twin = remote("g2_c", g2.at[1 - c], gs2, twin)
+    g2_twin.start()
+    qkv_bias_sum = col_sum(dxw[...].astype(F32))
+
+    for copy in g1_quad:
+        copy.wait_recv()
+
+    def quad_sum(i, carry):
+        rows = pl.ds(pl.multiple_of(i * 64, 64), 64)
+        at = pl.ds(pl.multiple_of(576 * s + i * 64, 64), 64)
+        x = gs1[h, at].astype(F32)
+        for k in range(3):
+            x = x + qr[k, rows].astype(F32)
+        gq[rows] = x.astype(BF)
+        return carry
+
+    lax.fori_loop(0, 576 // 64, quad_sum, 0)
+    zn1, zn2 = 576 // zc, 384 // zc
+
+    def chunk(t, n):
+        return pl.ds(pl.multiple_of(n * t, n), n)
+
+    z1 = [
+        remote("g1_z", gq.at[chunk(lax.rem(z + d, zc), zn1)], zr1.at[d - 1], z_peers[d - 1], d - 1, zc - 1)
+        for d in range(1, zc)
+    ]
+    for copy in z1:
+        copy.start()
+    g2_twin.wait_recv()
+    gs2[...] = (g2[c].astype(F32) + gs2[...].astype(F32)).astype(BF)
+    z2 = [
+        remote("g2_z", gs2.at[chunk(lax.rem(z + d, zc), zn2)], zr2.at[d - 1], z_peers[d - 1], d - 1, zc - 1)
+        for d in range(1, zc)
+    ]
+    for copy in z2:
+        copy.start()
+
+    wait_rows("fp", fp, fin)
+
+    def first_rows(rows, carry):
+        gain_sum, shift_sum = carry
+        fg = fin[0, rows].astype(F32)
+        for r in range(1, 4):
+            fg = fg + fin[r, rows].astype(F32)
+        n1, r1 = normed(res[rows].astype(F32))
+        g = fg * a_gain[...]
+        back = r1 * (
+            g - jnp.mean(g, axis=-1, keepdims=True) - n1 * jnp.mean(g * n1, axis=-1, keepdims=True)
+        )
+        at = pl.ds(pl.multiple_of(own + rows.start, 64), 64)
+        d_tok[at] = (mgd[rows] + back).astype(BF)
+        return gain_sum + col_sum(fg * n1), shift_sum + col_sum(fg)
+
+    a_gain_sum, a_shift_sum = row_loop(256, 64, first_rows, (zero_row, zero_row))
+    tok_send = remote("dtok", d_tok.at[own_rows], d_tok.at[own_rows], x_peer)
+    tok_send.start()
+
+    sums = [f_gain_sum, f_shift_sum, out_bias_sum, down_bias_sum, up_bias_sum, a_gain_sum, a_shift_sum, zero_row]
+    sums += [jnp.where(me == r, qkv_bias_sum, 0.0) for r in range(4)] + [zero_row] * 4
+    vq[me] = jnp.concatenate(sums, axis=0)
+    v1 = [remote("v_q", vq.at[me], vq.at[me], dev, k, 3) for k, dev in enumerate(quad)]
+    for copy in v1:
+        copy.start()
+
+    def finish(zs, dst_rows, own_part, parts, target):
+        for copy in zs:
+            copy.wait_recv()
+        x = own_part.astype(F32)
+        for d in range(zc - 1):
+            x = x + parts[d].astype(F32)
+        target[dst_rows] = x.astype(BF)
+
+    at1 = pl.ds(pl.multiple_of(576 * s + zn1 * z, 16), zn1)
+    at2 = pl.ds(pl.multiple_of(384 * c + zn2 * z, 16), zn2)
+    finish(z1, (c, at1), gq[chunk(z, zn1)], zr1, f1)
+    ag1 = [remote("f1_z", f1.at[c, at1], f1.at[c, at1], z_peers[d], d, zc - 1) for d in range(zc - 1)]
+    for copy in ag1:
+        copy.start()
+    finish(z2, (s, at2), gs2[chunk(z, zn2)], zr2, f2)
+    ag2 = [remote("f2_z", f2.at[s, at2], f2.at[s, at2], z_peers[d], d, zc - 1) for d in range(zc - 1)]
+    for copy in ag2:
+        copy.start()
+
+    v1_in = [
+        remote("v_q", vq.at[r], vq.at[r], dev, k, 3)
+        for k, (dev, r) in enumerate(zip(quad, (2 * s + 1 - h, 2 - 2 * s + h, 3 - 2 * s - h)))
+    ]
+    for copy in v1_in:
+        copy.wait_recv()
+    vz[z] = vq[0] + vq[1] + vq[2] + vq[3]
+    v2 = [remote("v_z", vz.at[z], vz.at[z], z_peers[d], d, zc - 1) for d in range(zc - 1)]
+    for copy in v2:
+        copy.start()
+
+    for copy in ag1:
+        copy.wait_recv()
+    half1 = half_of(s)
+    y1 = remote("f1_y", f1.at[c, half1], f1.at[c, half1], y_peer)
+    y1.start()
+    c1 = [remote("f1_c", f1.at[c, half1], f1.at[c, half1], twin, 0, 2)]
+    c1[0].start()
+    for copy in ag2:
+        copy.wait_recv()
+    half2 = pl.ds(pl.multiple_of(384 * c, 384), 384)
+    y2 = remote("f2_y", f2.at[s, half2], f2.at[s, half2], y_peer)
+    y2.start()
+    c2 = [remote("f2_c", f2.at[s, half2], f2.at[s, half2], twin, 0, 2)]
+    c2[0].start()
+    for copy in v2:
+        copy.wait_recv()
+    vsum = vz[0]
+    for d in range(1, zc):
+        vsum = vsum + vz[d]
+    vc[c] = vsum
+    v3 = remote("v_c", vc.at[c], vc.at[c], twin)
+    v3.start()
+    y1.wait_recv()
+    c1.append(remote("f1_c", f1.at[c, half_of(1 - s)], f1.at[c, half_of(1 - s)], twin, 1, 2))
+    c1[1].start()
+    y2.wait_recv()
+    c2.append(remote("f2_c", f2.at[1 - s, half2], f2.at[1 - s, half2], twin, 1, 2))
+    c2[1].start()
+    v3.wait_recv()
+    vec[...] = vc[0] + vc[1]
+    for copy in (*c1, *c2):
+        copy.wait_recv()
+    tok_send.wait_recv()
+    out_send.wait_recv()
+
+    @pl.when(s == 1)
+    def _():
+        for copy in tok_y:
+            copy.wait_send()
+
+    @pl.when(s == 0)
+    def _():
+        tok_n.wait_send()
+        for copy in tok_x:
+            copy.wait_send()
+
+    wait_sent("att", att, ain)
+    wait_sent("fp", fp, fin)
+    for k, (dev_sh, first, count) in enumerate(OWNERS):
+        mine = 2 * dev_sh[0] + dev_sh[1]
+
+        @pl.when(me == mine)
+        def _():
+            for r in range(4):
+                if r != mine:
+                    i = sem_id("da_s", 4) + r
+                    pltpu.make_async_remote_copy(
+                        src_ref=ago.at[0:count, 0:256], dst_ref=da.at[first:first + count],
+                        send_sem=ss.at[i], recv_sem=rs.at[i], device_id=x_peer, device_id_type=MESH,
+                    ).wait_send()
+
+    for copy in (
+        u_send, *w_out, *w_twin, out_send, g1_twin, *g1_quad, g2_twin, *z1, *z2, tok_send,
+        *v1, *ag1, *ag2, *v2, y1, y2, *c1, *c2, v3,
+    ):
+        copy.wait_send()
+
+
+def finish_kernel(
+    tokens, cot, d_out, d_tok, f1, f2, vec,
+    output, tokens_grad, a_gain, a_shift, wq, bq, wk, wv, bv, wo, bo, f_gain, f_shift, wu, bu, wd, bd,
+):
+    h = lax.axis_index("head")
+    output[...] = tokens[...].astype(F32) + d_out[...].astype(F32)
+    tokens_grad[...] = cot[...] + d_tok[...].astype(F32)
+    for k in range(2):
+        lanes = slice(384 * k, 384 * (k + 1))
+        wd[:, lanes] = f1[k, 0:384].astype(F32)
+        wo[:, lanes] = f1[k, 384:768].astype(F32)
+        wu[lanes, :] = f1[k, 768:1152].astype(F32)
+
+    def merge(a, b):
+        a, b = a.astype(F32), b.astype(F32)
+        return a[:, 0:128], a[:, 128:256] + b[:, 0:128], b[:, 128:256]
+
+    for k, out in enumerate((wq, wk, wv)):
+        cols = slice(256 * k, 256 * (k + 1))
+        for t, x in enumerate(merge(f2[0, :, cols], f2[1, :, cols])):
+            out[:, 128 * t:128 * (t + 1)] = x
+    mine = pl.ds(pl.multiple_of(384 * h, 384), 384)
+    for row, out in ((0, f_gain), (1, f_shift), (2, bo), (3, bd), (4, bu), (5, a_gain), (6, a_shift)):
+        out[...] = vec[row:row + 1, mine]
+    low = jnp.where(h == 0, vec[8:9], vec[9:10])
+    high = jnp.where(h == 0, vec[10:11], vec[11:12])
+    for first, out in ((0, bq), (512, bv)):
+        for t, x in enumerate(merge(low[:, first:first + 256], high[:, first:first + 256])):
+            out[:, 128 * t:128 * (t + 1)] = x
+
+
+def fast_layer(
+    tokens, cotangent, attn_gain, attn_shift, query_weight, query_bias, key_weight, value_weight,
+    value_bias, out_weight, out_bias, ffn_gain, ffn_shift, up_weight, up_bias, down_weight,
+    down_bias, atom_counts, edge_counts,
+):
+    zc = lax.axis_size("mol") // 2
+    row = lambda v: v.reshape(1, -1)
+    anywhere = pl.BlockSpec(memory_space=pl.ANY)
+    vmem = pl.BlockSpec(memory_space=pltpu.VMEM)
+    smem = pl.BlockSpec(memory_space=pltpu.SMEM)
+    shape = jax.ShapeDtypeStruct
+    SEM.clear()
+    buf = lambda dtype, *dims: pltpu.VMEM(dims, dtype)
+    scratch = [
+        buf(BF, PADDED, 768), buf(BF, 256, 768), buf(F32, 256, 768), buf(BF, 768, 768),
+        buf(BF, 2, 384, 768), buf(BF, 2, 768, 384), buf(BF, 2, 384, 768), buf(F32, 2, 8, 384),
+        buf(BF, PADDED, 768), buf(BF, PADDED, 768), buf(BF, TOTAL, 768),
+        buf(BF, HEADS_HERE, TOTAL, 256), buf(BF, HEADS_HERE, TOTAL, 256),
+        buf(BF, 2048, 640), buf(BF, 2048, 640), buf(BF, 1536, 768),
+        buf(F32, 256, 768), buf(jnp.int32, TOTAL, 1),
+        buf(F32, TOTAL, 256), buf(BF, TOTAL, 256), buf(BF, 4, 256, 256), buf(BF, TOTAL, 256), buf(F32, TOTAL, 128),
+        buf(F32, 256, 768), buf(F32, 256, 768), buf(F32, 256, 768), buf(F32, 256, 128), buf(F32, 256, 768),
+        buf(BF, 256, 768), buf(BF, 256, 768), buf(BF, 256, 768), buf(BF, 256, 768), buf(BF, 256, 768),
+        buf(BF, 256, 768), buf(BF, 256, 768), buf(F32, 256, 768),
+        buf(BF, 2048, 768), buf(F32, PADDED, 256), buf(F32, PADDED, 256),
+        buf(BF, 2, 2, 1152, 384), buf(BF, 2, 1152, 384), buf(BF, 3, 576, 384),
+        buf(BF, 576, 384), buf(BF, zc - 1, 576 // zc, 384),
+        buf(BF, 2, 384, 768), buf(BF, 384, 768), buf(BF, zc - 1, 384 // zc, 768),
+        buf(BF, TOTAL, 768), buf(BF, 4, 256, 768),
+        buf(F32, 4, 16, 768), buf(F32, zc, 16, 768), buf(F32, 2, 16, 768),
+        pltpu.SemaphoreType.DMA((N_SEMS,)), pltpu.SemaphoreType.DMA((N_SEMS,)), pltpu.SemaphoreType.DMA((N_LOCAL,)),
+    ]
+    d_out, d_tok, f1, f2, vec = pl.pallas_call(
+        layer_kernel,
+        out_shape=[
+            shape((512, 768), BF), shape((512, 768), BF), shape((2, 1152, 384), BF),
+            shape((2, 768, 768), BF), shape((16, 768), F32),
+        ],
+        in_specs=[anywhere] * 8 + [smem] * 2 + [vmem] * 9,
+        out_specs=[vmem] * 5,
+        scratch_shapes=scratch,
+        compiler_params=pltpu.CompilerParams(
+            collective_id=0, has_side_effects=True, vmem_limit_bytes=60 * 2**20
+        ),
+        name="layer",
+    )(
+        tokens, cotangent, query_weight, key_weight, value_weight, out_weight, up_weight, down_weight,
+        atom_counts, edge_counts,
+        row(attn_gain), row(attn_shift), row(query_bias), row(value_bias), row(out_bias),
+        row(ffn_gain), row(ffn_shift), row(up_bias), row(down_bias),
+    )
+    assert sum(n for _, n in SEM.values()) <= N_SEMS
+    mat, tall, line = shape((384, 768), F32), shape((768, 384), F32), shape((1, 384), F32)
+    big = shape((512, 768), F32)
+    outs = pl.pallas_call(
+        finish_kernel,
+        out_shape=[big, big, line, line, tall, line, tall, tall, line, mat, line, line, line, tall, line, mat, line],
+        in_specs=[vmem] * 7,
+        out_specs=[vmem] * 17,
+        compiler_params=pltpu.CompilerParams(vmem_limit_bytes=60 * 2**20),
+        name="finish",
+    )(tokens, cotangent, d_out, d_tok, f1, f2, vec)
+    return tuple(o.reshape(-1) if o.shape[0] == 1 else o for o in outs)
 
 
 def plain_dot(operand, partner):
@@ -34,7 +844,9 @@
 
 
 def segment_ids(counts, added, slot_count):
-    seg_ends = jnp.cumsum(counts + added)
+    members = jnp.arange(counts.shape[0])
+    earlier = members[:, None] <= members[None, :]
+    seg_ends = jnp.sum(jnp.where(earlier, (counts + added)[:, None], 0), axis=0)
     positions = jnp.arange(slot_count, dtype=jnp.int32)
     return jnp.sum((positions[:, None] >= seg_ends[None, :]).astype(jnp.int32), axis=1)
 
@@ -303,6 +1115,9 @@
         P("head", None),
         P("head"),
     )
+    one_chip_pair = (
+        mesh.shape["head"] == 2 and mesh.shape["stream"] == 2 and mesh.shape["mol"] == 8
+    )
     return jax.shard_map(
-        on_device, mesh=mesh, in_specs=in_specs, out_specs=out_specs, check_vma=False
-    )
+        fast_layer if one_chip_pair else on_device, mesh=mesh, in_specs=in_specs, out_specs=out_specs, check_vma=False
+    )

time: 566 us -> 187 us (0.33); the launches traced: 557 us -> 185 us
  waiting for transfers between devices: 239 us -> 0 us
  Pallas kernels: 0 us -> 161 us
  matrix products: 122 us -> 0 us
  blocking collectives: 88 us -> 0 us
  other arithmetic: 65.5 us -> 11.4 us
  between operations: 14.9 us -> 0.68 us
  starting transfers between devices: 9.47 us -> 0 us
  local copies, waits for them, and re-layouts: 18.6 us -> 11.3 us
    psum x4 -> x0, waiting for transfers between devices: 229 us -> none  [the longest x1 87.3 us: on_device(): lax.psum((attn_gain_grad, attn_shift_grad, query_weight_grad, query_bias_...]
    pallas_call x0 -> x2, Pallas kernels: none -> 161 us  [the longest x1 154 us: fast_layer(): pl.pallas_call(layer_kernel, out_shape=[shape((512, 768), BF), shape((512...]
    dot_general x24 -> x0, matrix products: 122 us -> none  [the longest x1 24.8 us: backward_block(): jnp.einsum('qhd,khd->hqk', grad_part, value_heads, preferred_element_type...]
    psum x1 -> x0, blocking collectives: 64 us -> none  [on_device(): lax.psum((attn_gain_grad, attn_shift_grad, query_weight_grad, query_bias_...]
    convert_element_type x6 -> x0, other arithmetic: 29.8 us -> none  [the longest x1 27.7 us: backward_block(): score_grad = (prob_full * (prob_grad - row_delta)).astype(jnp.bfloat16)]
    reduce_sum x12 -> x0, other arithmetic: 29 us -> none  [the longest x1 15.1 us: forward_block(): row_total = jnp.sum(shifted, axis=-1, keepdims=True)]
    all_gather x2 -> x0, blocking collectives: 24 us -> none  [the longest x1 12.9 us: on_device(): lax.all_gather(values_local, 'stream', axis=0, tiled=True)]
    unnamed x128 -> x0, local copies, waits for them, and re-layouts: 14.6 us -> none
  transfers between devices with their start and end apart: 6 -> 0, of which waited for: 5 -> 0; matrix products, arithmetic and copies ran while one was open for 10% -> 0% of each run, Pallas kernels for 0% -> 0%
where the time goes in v1:
time: 187 us; the launch traced here: 185 us
  Pallas kernels  161 us (86%)
  other arithmetic  11.4 us (6%)
  local copies, waits for them, and re-layouts  11.3 us (6%)
    pallas_call x1, Pallas kernels, fast_layer(): pl.pallas_call(layer_kernel, out_shape=[shape((512, 768), BF), shape((512...  154 us
    pallas_call x9, other arithmetic, fast_layer(): pl.pallas_call(finish_kernel, out_shape=[big, big, line, line, tall, line...  11.4 us
    reshape x9, local copies, waits for them, and re-layouts, fast_layer(): row = lambda v: v.reshape(1, -1)  11.3 us
    pallas_call x1, Pallas kernels, fast_layer(): pl.pallas_call(finish_kernel, out_shape=[big, big, line, line, tall, line...  7.36 us

profile of v1, /device:TPU:0, one launch (start us, length us, event | category | flops | bytes accessed | tf_op | source)
XLA Modules:
  0.0 184.9 jit_solution(449154039823054798)
XLA Ops:
  0.7 1.2 reshape.90.q_bias
  1.9 1.2 reshape.91.v_bias
  3.1 1.2 reshape.95.u_bias
  4.4 1.3 reshape.88.a_gain
  5.7 1.3 reshape.89.a_shift
  6.9 1.3 reshape.92.o_bias
  8.2 1.3 reshape.93.f_gain
  9.5 1.3 reshape.94.f_shift
  10.7 1.3 reshape.96.d_bias
  12.0 154.1 %layer.1 = (bf16[512,768]{1,0:T(8,128)(2,1)}, bf16[512,768]{1,0:T(8,128)(2,1)}, bf16[2,1152,384]{2,1,0:T(8,128)(2,1)}, bf16[2,768,768]{2,1,0:T(8,128)(2,1)}, f32[16,768]{1,0:T(8,128)}) custom-call(bf16[512,768]{1,0:T(8,128)(2,1)} %tokens.3, f32[512,768]{1,0:T(8,128)} %cot.3, bf16[768,384]{1,0:T(8,128)(2,1)} %wq.1, bf16[768,384]{1,0:T(8,128)(2,1)} %wk.1, ...), custom_call_target="tpu_custom_call" | custom-call | tf_op jit(solution)/shard_map/layer/pallas_call | solution.py:786
  166.1 7.4 %finish.1 = (f32[512,768]{1,0:T(8,128)}, f32[512,768]{1,0:T(8,128)}, f32[1,384]{1,0:T(1,128)}, f32[1,384]{1,0:T(1,128)}, f32[768,384]{1,0:T(8,128)}, /*index=5*/...) custom-call(bf16[512,768]{1,0:T(8,128)(2,1)} %tokens.3, ...), custom_call_target="tpu_custom_call" | custom-call | tf_op jit(solution)/shard_map/finish/pallas_call | solution.py:808
  173.5 1.3 reduce
  174.8 1.3 reduce.1
  176.0 1.3 reduce.2
  177.3 1.3 reduce.3
  178.6 1.3 reduce.4
  179.8 1.3 reduce.5
  181.1 1.3 reduce.6
  182.4 1.2 reduce.7
  183.6 1.3 reduce.8
